TPU v7x, 256 devices: a whole 4x4x8 slice. The times are simulated.
256 devices in a mesh: width: 8 (over z), hidden: 32 (over x, y, core).
Axes of the slice: x: 4, y: 4, z: 8, core: 2. Of those that a mesh axis runs over, the one named last changes fastest.
Arguments:
- tokens: bfloat16 [768, 16384], P('hidden', 'width'), may hold values from -6 to 6
- gate_weight: bfloat16 [16384, 28672], P('width', 'hidden'), may hold values from -0.046875 to 0.046875
- up_weight: bfloat16 [16384, 28672], P('width', 'hidden'), may hold values from -0.046875 to 0.046875
- down_weight: bfloat16 [28672, 16384], P('hidden', 'width'), may hold values from -0.03125 to 0.03125
Outputs:
- mixed: bfloat16 [768, 16384], P('hidden', 'width')
All inputs are finite; a program needn't handle non-finite values.
Results may differ from a plain program's by a relative error of at most 0.0049.
Values may be sent and summed in bfloat16 or wider, within the bound.
No kernel may reach another device: no remote copies, remote signals or barrier semaphores. Data moves between devices by JAX's collectives and lax.ppermute only.
A program may use at most 64 MiB of HBM per device.

v0:
```python
import jax
import jax.numpy as jnp
from jax import lax
from jax.sharding import PartitionSpec as P


def shards(tokens, gate_weight, up_weight, down_weight):
    piece = lax.all_gather(tokens, "hidden", axis=0, tiled=True)
    gate_part = jnp.dot(piece, gate_weight, preferred_element_type=jnp.float32)
    up_part = jnp.dot(piece, up_weight, preferred_element_type=jnp.float32)
    partial_terms = jnp.stack([gate_part, up_part])
    summed = lax.psum(partial_terms, "width")
    hidden_units = (jax.nn.silu(summed[0]) * summed[1]).astype(jnp.bfloat16)
    mixed = lax.psum_scatter(
        jnp.dot(hidden_units, down_weight, preferred_element_type=jnp.float32),
        "hidden",
        scatter_dimension=0,
        tiled=True,
    )
    return mixed.astype(jnp.bfloat16)


def solution(mesh):
    return jax.shard_map(
        shards,
        mesh=mesh,
        in_specs=(
            P("hidden", "width"),
            P("width", "hidden"),
            P("width", "hidden"),
            P("hidden", "width"),
        ),
        out_specs=P("hidden", "width"),
        check_vma=False,
    )
```

profile of v0, /device:TPU:24, one launch (start us, length us, event | category | flops | bytes accessed | tf_op | source)
XLA Modules:
  0.0 319.1 jit_solution(1199477574434476446)
XLA Ops:
  6.5 0.0 all-gather.2.cloned.1.call-start
  6.5 0.7 all-gather.2.cloned.1.call-update
  7.3 0.0 all-reduce.2.cloned.1.call-start
  7.3 55.0 %all-gather.2.cloned.1.call-done = bf16[768,2048]{1,0:T(8,128)(2,1)} async-done(((bf16[24,2048]{1,0:T(8,128)(2,1)}), bf16[768,2048]{1,0:T(8,128)(2,1)}) %all-gather.2.cloned.1.call-update) | async-done | bytes 3145744 | tf_op jit(solution)/shard_map/all_gather | solution.py:8
  62.3 0.0 copy-start
  62.3 0.0 copy-start.1
  62.3 6.5 %convolution_bitcast_fusion = f32[1,768,896]{2,1,0:T(8,128)S(1)} fusion(bf16[768,2048]{1,0:T(8,128)(2,1)} %all-gather.2.cloned.1.call-done, bf16[2048,896]{1,0:T(8,128)(2,1)} %param.6), kind=kOutput, calls=%fused_computation.5 | convolution fusion | flops 2818572288 | bytes 9568256 | tf_op jit(solution)/shard_map/dot_general | solution.py:10
  68.8 0.0 copy-done
  68.8 0.0 copy-done.1
  68.8 3.4 %convolution_bitcast_fusion.1 = f32[1,768,896]{2,1,0:T(8,128)S(1)} fusion(bf16[768,2048]{1,0:T(8,128)(2,1)S(1)} %copy-done.1, bf16[2048,896]{1,0:T(8,128)(2,1)S(1)} %copy-done), kind=kOutput, calls=%fused_computation.6 | convolution fusion | flops 2818572288 | bytes 9568256 | tf_op jit(solution)/shard_map/dot_general | solution.py:9
  72.2 2.8 pad_maximum_fusion
  75.0 0.0 all-reduce.2.cloned.1.call-update
  75.0 0.0 reduce-scatter.2.cloned.1.call-start
  75.1 133.7 %all-reduce.2.cloned.1.call-done = f32[2,768,896]{2,1,0:T(8,128)} async-done(((f32[2,768,896]{2,1,0:T(8,128)}), f32[2,768,896]{2,1,0:T(8,128)}) %all-reduce.2.cloned.1.call-update) | async-done | bytes 5505040 | tf_op jit(solution)/shard_map/psum | solution.py:12
  208.7 9.8 %fusion.2 = f32[768,2048]{1,0:T(8,128)} fusion(bf16[896,2048]{1,0:T(8,128)(2,1)} %param.7, f32[2,768,896]{2,1,0:T(8,128)} %all-reduce.2.cloned.1.call-done), kind=kOutput, calls=%fused_computation.7 | convolution fusion | flops 2822701056 | bytes 15466496 | tf_op jit(solution)/shard_map/dot_general | solution.py:15
  218.5 0.0 reduce-scatter.2.cloned.1.call-update
  218.5 92.4 %reduce-scatter.2.cloned.1.call-done = f32[24,2048]{1,0:T(8,128)} async-done(((f32[768,2048]{1,0:T(8,128)}), f32[24,2048]{1,0:T(8,128)}) %reduce-scatter.2.cloned.1.call-update) | async-done | bytes 196624 | tf_op jit(solution)/shard_map/reduce_scatter | solution.py:14
  311.0 1.6 convert_element_type.7
Async XLA Ops:
  6.5 55.7 %all-gather.2.cloned.1.call-start = ((), (), s32[]{:S(2)}) async-start(), calls=%async_computation.1 | async-start | bytes 3244032 | tf_op jit(solution)/shard_map/all_gather | solution.py:8
  7.3 201.5 %all-reduce.2.cloned.1.call-start = ((), (), s32[]{:S(2)}) async-start(), calls=%async_computation.2 | async-start | bytes 11010048 | tf_op jit(solution)/shard_map/psum | solution.py:12
  62.3 6.5 %copy-start = (bf16[2048,896]{1,0:T(8,128)(2,1)S(1)}, bf16[2048,896]{1,0:T(8,128)(2,1)}, u32[]{:S(2)}) copy-start(bf16[2048,896]{1,0:T(8,128)(2,1)} %param.5) | copy-start | bytes 11010052
  62.3 6.6 %copy-start.1 = (bf16[768,2048]{1,0:T(8,128)(2,1)S(1)}, bf16[768,2048]{1,0:T(8,128)(2,1)}, u32[]{:S(2)}) copy-start(bf16[768,2048]{1,0:T(8,128)(2,1)} %all-gather.2.cloned.1.call-done) | copy-start | bytes 9437188
  75.0 235.9 %reduce-scatter.2.cloned.1.call-start = ((), (), s32[]{:S(2)}) async-start(), calls=%async_computation.3 | async-start | bytes 6488064 | tf_op jit(solution)/shard_map/reduce_scatter | solution.py:14
Sparse Core Ops, SparseCore 0:
  9.9 52.3 all-gather.1
  75.1 133.5 all-reduce.1
  218.6 92.2 reduce-scatter.1
where the time goes:
time: 319 us
  waiting for transfers between devices  282 us (88%)
  matrix products  19.7 us (6%)
  between operations  13.1 us (4%)
  other arithmetic  4.33 us (1%)
    psum x1, waiting for transfers between devices, shards(): summed = lax.psum(partial_terms, 'width')  134 us
    reduce_scatter x1, waiting for transfers between devices, shards(): lax.psum_scatter(jnp.dot(hidden_units, down_weight, preferred_element_typ...  92.4 us
    all_gather x1, waiting for transfers between devices, shards(): piece = lax.all_gather(tokens, 'hidden', axis=0, tiled=True)  55 us
    dot_general x1, matrix products, shards(): jnp.dot(hidden_units, down_weight, preferred_element_type=jnp.float32)  9.78 us
    dot_general x1, matrix products, shards(): up_part = jnp.dot(piece, up_weight, preferred_element_type=jnp.float32)  6.53 us
  transfers between devices with their start and end apart: 3, of which 3 were waited for; matrix products, arithmetic and copies ran while one was open for 0% of the time, Pallas kernels for 0%

commit v1 on v0

v1 whole, which is shorter than its diff:
```python
import jax
import jax.numpy as jnp
from jax import lax
from jax.sharding import PartitionSpec as P

W = "width"
H = "hidden"
NX = NY = 4
NZ = 8
BF = jnp.bfloat16
F16 = jnp.float16
F32 = jnp.float32


def place(x, y, c):
    return (x % NX * NY + y % NY) * 2 + c % 2


def moved(axis, d):
    pairs = []
    for x in range(NX):
        for y in range(NY):
            for c in range(2):
                along_x = (c == 0) == (axis == 0)
                to = place(x + d, y, c) if along_x else place(x, y + d, c)
                pairs.append((place(x, y, c), to))
    return pairs


SWAP = [(h, h ^ 1) for h in range(2 * NX * NY)]


def turn(d):
    return [(i, (i + d) % NZ) for i in range(NZ)]


def scale_of(tokens, gate_weight, up_weight):
    largest = jnp.stack(
        [
            jnp.max(jnp.abs(tokens)).astype(F32),
            jnp.maximum(jnp.max(jnp.abs(gate_weight)), jnp.max(jnp.abs(up_weight))).astype(F32),
        ]
    )
    largest = lax.pmax(largest, (H, W))
    bound = jnp.maximum(largest[0], 1e-12) * jnp.maximum(largest[1], 1e-12) * (NZ * gate_weight.shape[0])
    return 32768.0 / bound, bound * (1.0 / 32768.0)


def summed_over_width(part, z, scale):
    rows = part.shape[1] // 2

    def own(k, lo, hi):
        chunk = lax.dynamic_index_in_dim(part, lax.rem(z + k + NZ, NZ), 0, keepdims=False)
        return chunk[lo:hi] * scale

    full = part.shape[1]
    up = lax.ppermute(own(4, 0, rows).astype(F16), W, turn(1))
    down = lax.ppermute(own(-4, rows, full).astype(F16), W, turn(-1))
    for k in (3, 2, 1):
        if k == 3:
            send_up = jnp.concatenate([up.astype(F32) + own(3, 0, rows), own(3, rows, full)])
            send_down = jnp.concatenate([own(-3, 0, rows), down.astype(F32) + own(-3, rows, full)])
        else:
            send_up = up.astype(F32) + own(k, 0, full)
            send_down = down.astype(F32) + own(-k, 0, full)
        up = lax.ppermute(send_up.astype(F16), W, turn(1))
        down = lax.ppermute(send_down.astype(F16), W, turn(-1))
    return up.astype(F32) + down.astype(F32) + own(0, 0, full)


def gathered_over_width(own, z):
    rows = own.shape[0] // 2
    out = jnp.zeros((NZ,) + own.shape, own.dtype)

    def put(out, block, k):
        return lax.dynamic_update_slice(out, block[None], (lax.rem(z + k + NZ, NZ), 0, 0))

    out = put(out, own, 0)
    up = down = own
    for k in (1, 2, 3):
        up = lax.ppermute(up, W, turn(1))
        down = lax.ppermute(down, W, turn(-1))
        out = put(put(out, up, -k), down, k)
    far = jnp.concatenate(
        [lax.ppermute(up[:rows], W, turn(1)), lax.ppermute(down[rows:], W, turn(-1))]
    )
    return put(out, far, 4)


def shards(tokens, gate_weight, up_weight, down_weight):
    z = lax.axis_index(W)
    mine = tokens.shape[0]
    scale, unscale = scale_of(tokens, gate_weight, up_weight)

    line = jnp.concatenate([tokens] + [lax.ppermute(tokens, H, moved(0, -d)) for d in (1, 2, 3)])
    plane = jnp.concatenate([line] + [lax.ppermute(line, H, moved(1, -d)) for d in (1, 2, 3)])
    piece = jnp.concatenate([plane, lax.ppermute(plane, H, SWAP)])

    chunks = (NZ, piece.shape[0] // NZ, gate_weight.shape[1])
    gate_part = jnp.dot(piece, gate_weight, preferred_element_type=F32).reshape(chunks)
    up_part = jnp.dot(piece, up_weight, preferred_element_type=F32).reshape(chunks)
    gate = summed_over_width(gate_part, z, scale) * unscale
    up = summed_over_width(up_part, z, scale) * unscale
    hidden_units = gathered_over_width((jax.nn.silu(gate) * up).astype(BF), z)

    terms = jnp.dot(hidden_units.reshape(piece.shape[0], -1), down_weight, preferred_element_type=F32)
    half = terms.shape[0] // 2
    total = terms[:half] + lax.ppermute(terms[half:].astype(BF), H, SWAP).astype(F32)
    for axis in (1, 0):
        rows = total.shape[0] // 4
        sent = [lax.ppermute(total[d * rows : (d + 1) * rows].astype(BF), H, moved(axis, d)) for d in (1, 2, 3)]
        total = total[:rows] + sent[0].astype(F32) + sent[1].astype(F32) + sent[2].astype(F32)
    return total.astype(BF)


def solution(mesh):
    return jax.shard_map(
        shards,
        mesh=mesh,
        in_specs=(
            P(H, W),
            P(W, H),
            P(W, H),
            P(H, W),
        ),
        out_specs=P(H, W),
        check_vma=False,
    )
```

time: 319 us -> 238 us (0.75); the launches traced: 319 us -> 234 us
  waiting for transfers between devices: 282 us -> 57.8 us
  blocking collectives: 0 us -> 78.7 us
  starting transfers between devices: 0.08 us -> 65.6 us
  between operations: 13.1 us -> 3.18 us
  other arithmetic: 4.33 us -> 10.8 us
  matrix products: 19.7 us -> 13.3 us
  local copies, waits for them, and re-layouts: 0.01 us -> 4.29 us
    psum x1 -> x0, waiting for transfers between devices: 134 us -> none  [shards(): summed = lax.psum(partial_terms, 'width')]
    reduce_scatter x1 -> x0, waiting for transfers between devices: 92.4 us -> none  [shards(): lax.psum_scatter(jnp.dot(hidden_units, down_weight, preferred_element_typ...]
    pmax x0 -> x1, blocking collectives: none -> 78.7 us  [scale_of(): largest = lax.pmax(largest, (H, W))]
    ppermute x0 -> x38, starting transfers between devices: none -> 65.6 us  [the longest x6 19.1 us: summed_over_width(): down = lax.ppermute(send_down.astype(F16), W, turn(-1))]
    ppermute x0 -> x38, waiting for transfers between devices: none -> 57.8 us  [the longest x6 17.5 us: shards(): lax.ppermute(total[d * rows:(d + 1) * rows].astype(BF), H, moved(axis, d))]
    all_gather x1 -> x0, waiting for transfers between devices: 55 us -> none  [shards(): piece = lax.all_gather(tokens, 'hidden', axis=0, tiled=True)]
    dot_general x3, matrix products: 19.7 us -> 13.3 us  [the longest x1 6.53 us: shards(): jnp.dot(piece, up_weight, preferred_element_type=F32).reshape(chunks)]
    reduce_max x0 -> x2, other arithmetic: none -> 5.25 us  [the longest x1 3.66 us: scale_of(): jnp.max(jnp.abs(up_weight))]
  transfers between devices with their start and end apart: 3 -> 38, of which waited for: 3 -> 20; matrix products, arithmetic and copies ran while one was open for 0% -> 4% of each run, Pallas kernels for 0% -> 0%
where the time goes in v1:
time: 238 us; the launch traced here: 234 us
  blocking collectives  78.7 us (33%)
  starting transfers between devices  65.6 us (28%)
  waiting for transfers between devices  57.8 us (24%)
  matrix products  13.3 us (6%)
  other arithmetic  10.8 us (5%)
  local copies, waits for them, and re-layouts  4.29 us (2%)
  between operations  3.18 us (1%)
    pmax x1, blocking collectives, scale_of(): largest = lax.pmax(largest, (H, W))  78.7 us
    ppermute x6, starting transfers between devices, summed_over_width(): down = lax.ppermute(send_down.astype(F16), W, turn(-1))  19.1 us
    ppermute x6, waiting for transfers between devices, shards(): lax.ppermute(total[d * rows:(d + 1) * rows].astype(BF), H, moved(axis, d))  17.5 us
    ppermute x3, waiting for transfers between devices, gathered_over_width(): up = lax.ppermute(up, W, turn(1))  11.6 us
    ppermute x3, starting transfers between devices, gathered_over_width(): up = lax.ppermute(up, W, turn(1))  10.3 us
    ppermute x3, waiting for transfers between devices, shards(): lax.ppermute(line, H, moved(1, -d))  10.1 us
    ppermute x3, starting transfers between devices, gathered_over_width(): down = lax.ppermute(down, W, turn(-1))  9.51 us
    ppermute x6, waiting for transfers between devices, summed_over_width(): up = lax.ppermute(send_up.astype(F16), W, turn(1))  8.79 us
  transfers between devices with their start and end apart: 38, of which 20 were waited for; matrix products, arithmetic and copies ran while one was open for 4% of the time, Pallas kernels for 0%

profile of v1, /device:TPU:24, one launch (start us, length us, event | category | flops | bytes accessed | tf_op | source)
XLA Modules:
  0.0 233.7 jit_solution(12207562771481231804)
XLA Ops:
  0.0 3.0 %collective-permute-start.1 = (bf16[24,2048]{1,0:T(8,128)(2,1)}, bf16[24,2048]{1,0:T(8,128)(2,1)S(1)}, u32[]{:S(2)}, u32[]{:S(2)}) collective-permute-start(bf16[24,2048]{1,0:T(8,128)(2,1)} %param.4), channel_id=1, source_target_pairs={{0,16},{1,5},{2,18},{3,7},{4,20},{5,1},{6,22},{7,3},{8,24},{9,13},... | collective-permute-start | bytes 294920 | tf_op jit(solution)/shard_map/ppermute | solution.py:95
  3.0 1.1 collective-permute-start
  4.2 0.9 collective-permute-start.2
  5.1 1.6 abs_reduce_fusion.2
  6.6 1.2 collective-permute-done
  7.9 2.3 collective-permute-done.2
  10.2 0.8 collective-permute-start.3
  11.1 0.9 collective-permute-start.4
  12.0 2.2 collective-permute-start.5
  14.2 9.3 %collective-permute-done.3 = bf16[96,2048]{1,0:T(8,128)(2,1)S(1)} collective-permute-done((bf16[96,2048]{1,0:T(8,128)(2,1)S(1)}, bf16[96,2048]{1,0:T(8,128)(2,1)S(1)}, u32[]{:S(2)}, u32[]{:S(2)}) %collective-permute-start.3) | collective-permute-done | bytes 393248 | tf_op jit(solution)/shard_map/ppermute | solution.py:96
  23.6 0.8 collective-permute-done.5
  24.5 1.6 copy-done.3
  26.1 3.7 %abs_reduce_fusion = (bf16[]{:T(256)}, bf16[]{:T(256)}) fusion(bf16[2048,896]{1,0:T(8,128)(2,1)S(1)} %copy-done, bf16[2048,896]{1,0:T(8,128)(2,1)} %param.5), kind=kLoop, calls=%fused_computation | loop fusion | flops 7340030 | bytes 7340036 | tf_op jit(solution)/shard_map/reduce_max | solution.py:41
  31.0 0.7 maximum_convert_fusion
  31.8 78.7 %pmax.7 = f32[2]{0:T(128)S(1)} all-reduce(f32[2]{0:T(128)S(1)} %maximum_convert_fusion), channel_id=1, replica_groups=mesh['width'=8,'hidden'=32] {'hidden','width'}, use_global_device_ids=true, to_apply=%region_3.0 | all-reduce | flops 2 | bytes 16 | tf_op jit(solution)/shard_map/pmax | solution.py:44
  110.4 0.6 fusion.52
  112.4 1.2 constant_dynamic-update-slice_fusion.11
  113.7 6.5 %fusion.54 = f32[768,896]{1,0:T(8,128)S(1)} fusion(bf16[768,2048]{1,0:T(8,128)(2,1)} %constant_dynamic-update-slice_fusion.11, bf16[2048,896]{1,0:T(8,128)(2,1)} %param.6), kind=kOutput, calls=%fused_computation.113 | convolution fusion | flops 2818572288 | bytes 9568256 | tf_op jit(solution)/shard_map/dot_general | solution.py:101
  120.2 3.4 %fusion.53 = f32[768,896]{1,0:T(8,128)S(1)} fusion(bf16[768,2048]{1,0:T(8,128)(2,1)S(1)} %copy-done.4, bf16[2048,896]{1,0:T(8,128)(2,1)S(1)} %copy-done.1), kind=kOutput, calls=%fused_computation.112 | convolution fusion | flops 2818572288 | bytes 9568256 | tf_op jit(solution)/shard_map/dot_general | solution.py:100
  123.7 1.1 collective-permute-start.15
  124.8 2.5 %collective-permute-start.19 = (f16[48,896]{1,0:T(8,128)(2,1)S(1)}, f16[48,896]{1,0:T(8,128)(2,1)S(1)}, u32[]{:S(2)}, u32[]{:S(2)}) collective-permute-start(f16[48,896]{1,0:T(8,128)(2,1)S(1)} %get-tuple-element.29), channel_id=1, source_target_pairs={{0,224},{32,0},{64,32},{96,64},{128,96},{160,128},{192,160},{224,1... | collective-permute-start | bytes 258056 | tf_op jit(solution)/shard_map/ppermute | solution.py:58
  127.4 3.2 %collective-permute-start.11 = (f16[48,896]{1,0:T(8,128)(2,1)S(1)}, f16[48,896]{1,0:T(8,128)(2,1)S(1)}, u32[]{:S(2)}, u32[]{:S(2)}) collective-permute-start(f16[48,896]{1,0:T(8,128)(2,1)S(1)} %get-tuple-element.19), channel_id=1, source_target_pairs={{0,224},{32,0},{64,32},{96,64},{128,96},{160,128},{192,160},{224,1... | collective-permute-start | bytes 258056 | tf_op jit(solution)/shard_map/ppermute | solution.py:58
  130.8 2.4 %collective-permute-start.20 = (f16[96,896]{1,0:T(8,128)(2,1)S(1)}, f16[96,896]{1,0:T(8,128)(2,1)S(1)}, u32[]{:S(2)}, u32[]{:S(2)}) collective-permute-start(f16[96,896]{1,0:T(8,128)(2,1)S(1)} %pad_maximum_fusion.3), channel_id=1, source_target_pairs={{0,224},{32,0},{64,32},{96,64},{128,96},{160,128},{192,160},{224,1... | collective-permute-start | bytes 516104 | tf_op jit(solution)/shard_map/ppermute | solution.py:67
  133.3 0.3 collective-permute-done.11
  133.7 3.8 %collective-permute-start.12 = (f16[96,896]{1,0:T(8,128)(2,1)S(1)}, f16[96,896]{1,0:T(8,128)(2,1)S(1)}, u32[]{:S(2)}, u32[]{:S(2)}) collective-permute-start(f16[96,896]{1,0:T(8,128)(2,1)S(1)} %pad_maximum_fusion.1), channel_id=1, source_target_pairs={{0,224},{32,0},{64,32},{96,64},{128,96},{160,128},{192,160},{224,1... | collective-permute-start | bytes 516104 | tf_op jit(solution)/shard_map/ppermute | solution.py:67
  137.6 0.3 collective-permute-done.20
  137.9 3.7 %collective-permute-done.16 = f16[96,896]{1,0:T(8,128)(2,1)S(1)} collective-permute-done((f16[96,896]{1,0:T(8,128)(2,1)S(1)}, f16[96,896]{1,0:T(8,128)(2,1)S(1)}, u32[]{:S(2)}, u32[]{:S(2)}) %collective-permute-start.16) | collective-permute-done | bytes 172064 | tf_op jit(solution)/shard_map/ppermute | solution.py:66
  141.6 0.1 fusion.8
  141.8 3.2 %collective-permute-start.21 = (f16[96,896]{1,0:T(8,128)(2,1)S(1)}, f16[96,896]{1,0:T(8,128)(2,1)S(1)}, u32[]{:S(2)}, u32[]{:S(2)}) collective-permute-start(f16[96,896]{1,0:T(8,128)(2,1)S(1)} %get-tuple-element.24), channel_id=1, source_target_pairs={{0,224},{32,0},{64,32},{96,64},{128,96},{160,128},{192,160},{224,1... | collective-permute-start | bytes 516104 | tf_op jit(solution)/shard_map/ppermute | solution.py:67
  145.0 0.4 collective-permute-done.8
  145.4 0.1 fusion.13
  145.6 3.2 %collective-permute-start.13 = (f16[96,896]{1,0:T(8,128)(2,1)S(1)}, f16[96,896]{1,0:T(8,128)(2,1)S(1)}, u32[]{:S(2)}, u32[]{:S(2)}) collective-permute-start(f16[96,896]{1,0:T(8,128)(2,1)S(1)} %get-tuple-element.14), channel_id=1, source_target_pairs={{0,224},{32,0},{64,32},{96,64},{128,96},{160,128},{192,160},{224,1... | collective-permute-start | bytes 516104 | tf_op jit(solution)/shard_map/ppermute | solution.py:67
  148.9 1.0 collective-permute-done.17
  150.1 3.2 %collective-permute-start.22 = (f16[96,896]{1,0:T(8,128)(2,1)S(1)}, f16[96,896]{1,0:T(8,128)(2,1)S(1)}, u32[]{:S(2)}, u32[]{:S(2)}) collective-permute-start(f16[96,896]{1,0:T(8,128)(2,1)S(1)} %get-tuple-element.22), channel_id=1, source_target_pairs={{0,224},{32,0},{64,32},{96,64},{128,96},{160,128},{192,160},{224,1... | collective-permute-start | bytes 516104 | tf_op jit(solution)/shard_map/ppermute | solution.py:67
  153.3 0.8 fusion.12
  154.2 3.2 %collective-permute-start.14 = (f16[96,896]{1,0:T(8,128)(2,1)}, f16[96,896]{1,0:T(8,128)(2,1)}, u32[]{:S(2)}, u32[]{:S(2)}) collective-permute-start(f16[96,896]{1,0:T(8,128)(2,1)} %get-tuple-element.12), channel_id=1, source_target_pairs={{0,224},{32,0},{64,32},{96,64},{128,96},{160,128},{192,160},{224,1... | collective-permute-start | bytes 516104 | tf_op jit(solution)/shard_map/ppermute | solution.py:67
  157.4 3.7 %collective-permute-done.10 = f16[96,896]{1,0:T(8,128)(2,1)} collective-permute-done((f16[96,896]{1,0:T(8,128)(2,1)}, f16[96,896]{1,0:T(8,128)(2,1)}, u32[]{:S(2)}, u32[]{:S(2)}) %collective-permute-start.10) | collective-permute-done | bytes 172064 | tf_op jit(solution)/shard_map/ppermute | solution.py:66
  161.2 1.5 bitcast_dynamic-update-slice_fusion.6
  162.7 10.3 %collective-permute-start.23 = (bf16[96,896]{1,0:T(8,128)(2,1)S(1)}, bf16[96,896]{1,0:T(8,128)(2,1)S(1)}, u32[]{:S(2)}, u32[]{:S(2)}) collective-permute-start(bf16[96,896]{1,0:T(8,128)(2,1)S(1)} %get-tuple-element.10), channel_id=1, source_target_pairs={{0,32},{32,64},{64,96},{96,128},{128,160},{160,192},{192,224},{224... | collective-permute-start | bytes 516104 | tf_op jit(solution)/shard_map/ppermute | solution.py:81
  173.0 2.9 %collective-permute-start.24 = (bf16[96,896]{1,0:T(8,128)(2,1)S(1)}, bf16[96,896]{1,0:T(8,128)(2,1)S(1)}, u32[]{:S(2)}, u32[]{:S(2)}) collective-permute-start(bf16[96,896]{1,0:T(8,128)(2,1)S(1)} %get-tuple-element.10), channel_id=1, source_target_pairs={{0,224},{32,0},{64,32},{96,64},{128,96},{160,128},{192,160},{224,1... | collective-permute-start | bytes 516104 | tf_op jit(solution)/shard_map/ppermute | solution.py:82
  175.9 4.6 %collective-permute-done.23 = bf16[96,896]{1,0:T(8,128)(2,1)S(1)} collective-permute-done((bf16[96,896]{1,0:T(8,128)(2,1)S(1)}, bf16[96,896]{1,0:T(8,128)(2,1)S(1)}, u32[]{:S(2)}, u32[]{:S(2)}) %collective-permute-start.23) | collective-permute-done | bytes 172064 | tf_op jit(solution)/shard_map/ppermute | solution.py:81
  180.5 3.3 %collective-permute-start.26 = (bf16[96,896]{1,0:T(8,128)(2,1)S(1)}, bf16[96,896]{1,0:T(8,128)(2,1)S(1)}, u32[]{:S(2)}, u32[]{:S(2)}) collective-permute-start(bf16[96,896]{1,0:T(8,128)(2,1)S(1)} %collective-permute-done.24), channel_id=1, source_target_pairs={{0,224},{32,0},{64,32},{96,64},{128,96},{160,128},{192,160},{224,1... | collective-permute-start | bytes 516104 | tf_op jit(solution)/shard_map/ppermute | solution.py:82
  183.8 3.8 %collective-permute-done.25 = bf16[96,896]{1,0:T(8,128)(2,1)S(1)} collective-permute-done((bf16[96,896]{1,0:T(8,128)(2,1)S(1)}, bf16[96,896]{1,0:T(8,128)(2,1)S(1)}, u32[]{:S(2)}, u32[]{:S(2)}) %collective-permute-start.25) | collective-permute-done | bytes 172064 | tf_op jit(solution)/shard_map/ppermute | solution.py:81
  187.6 3.3 %collective-permute-start.28 = (bf16[96,896]{1,0:T(8,128)(2,1)S(1)}, bf16[96,896]{1,0:T(8,128)(2,1)S(1)}, u32[]{:S(2)}, u32[]{:S(2)}) collective-permute-start(bf16[96,896]{1,0:T(8,128)(2,1)S(1)} %collective-permute-done.26), channel_id=1, source_target_pairs={{0,224},{32,0},{64,32},{96,64},{128,96},{160,128},{192,160},{224,1... | collective-permute-start | bytes 516104 | tf_op jit(solution)/shard_map/ppermute | solution.py:82
  191.0 3.2 %collective-permute-done.27 = bf16[96,896]{1,0:T(8,128)(2,1)S(1)} collective-permute-done((bf16[96,896]{1,0:T(8,128)(2,1)S(1)}, bf16[96,896]{1,0:T(8,128)(2,1)S(1)}, u32[]{:S(2)}, u32[]{:S(2)}) %collective-permute-start.27) | collective-permute-done | bytes 172064 | tf_op jit(solution)/shard_map/ppermute | solution.py:81
  194.3 3.3 %collective-permute-start.30 = (bf16[48,896]{1,0:T(8,128)(2,1)S(1)}, bf16[48,896]{1,0:T(8,128)(2,1)S(1)}, u32[]{:S(2)}, u32[]{:S(2)}) collective-permute-start(bf16[48,896]{1,0:T(8,128)(2,1)S(1)} %slice.124), channel_id=1, source_target_pairs={{0,224},{32,0},{64,32},{96,64},{128,96},{160,128},{192,160},{224,1... | collective-permute-start | bytes 258056 | tf_op jit(solution)/shard_map/ppermute | solution.py:85
  197.7 2.3 collective-permute-done.29
  200.0 3.4 %fusion.55 = f32[768,2048]{1,0:T(8,128)S(1)} fusion(bf16[768,896]{1,0:T(8,128)(2,1)S(1)} %bitcast.129, bf16[896,2048]{1,0:T(8,128)(2,1)S(1)} %copy-done.5), kind=kOutput, calls=%fused_computation.114 | convolution fusion | flops 2818572288 | bytes 11337728 | tf_op jit(solution)/shard_map/dot_general | solution.py:106
  203.5 0.2 slice.149
  203.8 3.4 %collective-permute-done.31 = bf16[384,2048]{1,0:T(8,128)(2,1)S(1)} collective-permute-done((bf16[384,2048]{1,0:T(8,128)(2,1)S(1)}, bf16[384,2048]{1,0:T(8,128)(2,1)S(1)}, u32[]{:S(2)}, u32[]{:S(2)}) %collective-permute-start.31) | collective-permute-done | bytes 1572896 | tf_op jit(solution)/shard_map/ppermute | solution.py:108
  207.2 0.8 fusion.48
  208.0 1.9 collective-permute-start.32
  210.0 0.2 collective-permute-start.34
  210.1 1.4 collective-permute-start.33
  211.5 8.0 %collective-permute-done.32 = bf16[96,2048]{1,0:T(8,128)(2,1)S(1)} collective-permute-done((bf16[96,2048]{1,0:T(8,128)(2,1)S(1)}, bf16[96,2048]{1,0:T(8,128)(2,1)S(1)}, u32[]{:S(2)}, u32[]{:S(2)}) %collective-permute-start.32) | collective-permute-done | bytes 393248 | tf_op jit(solution)/shard_map/ppermute | solution.py:111
  219.5 3.7 %collective-permute-done.34 = bf16[96,2048]{1,0:T(8,128)(2,1)S(1)} collective-permute-done((bf16[96,2048]{1,0:T(8,128)(2,1)S(1)}, bf16[96,2048]{1,0:T(8,128)(2,1)S(1)}, u32[]{:S(2)}, u32[]{:S(2)}) %collective-permute-start.34) | collective-permute-done | bytes 393248 | tf_op jit(solution)/shard_map/ppermute | solution.py:111
  223.2 0.2 fusion.46
  223.4 0.2 collective-permute-start.35
  223.6 3.1 %collective-permute-start.37 = (bf16[24,2048]{1,0:T(8,128)(2,1)S(1)}, bf16[24,2048]{1,0:T(8,128)(2,1)S(1)}, u32[]{:S(2)}, u32[]{:S(2)}) collective-permute-start(bf16[24,2048]{1,0:T(8,128)(2,1)S(1)} %get-tuple-element.35), channel_id=1, source_target_pairs={{0,24},{1,7},{2,26},{3,1},{4,28},{5,3},{6,30},{7,5},{8,0},{9,15},{... | collective-permute-start | bytes 294920 | tf_op jit(solution)/shard_map/ppermute | solution.py:111
  226.7 0.2 collective-permute-start.36
  227.0 2.3 %collective-permute-done.35 = bf16[24,2048]{1,0:T(8,128)(2,1)S(1)} collective-permute-done((bf16[24,2048]{1,0:T(8,128)(2,1)S(1)}, bf16[24,2048]{1,0:T(8,128)(2,1)S(1)}, u32[]{:S(2)}, u32[]{:S(2)}) %collective-permute-start.35) | collective-permute-done | bytes 98336 | tf_op jit(solution)/shard_map/ppermute | solution.py:111
  229.3 0.6 collective-permute-done.37
  230.0 2.9 %collective-permute-done.36 = bf16[24,2048]{1,0:T(8,128)(2,1)S(1)} collective-permute-done((bf16[24,2048]{1,0:T(8,128)(2,1)S(1)}, bf16[24,2048]{1,0:T(8,128)(2,1)S(1)}, u32[]{:S(2)}, u32[]{:S(2)}) %collective-permute-start.36) | collective-permute-done | bytes 98336 | tf_op jit(solution)/shard_map/ppermute | solution.py:111
  232.9 0.7 fusion.16
  (68 shorter events, 1.9 us)
Async XLA Ops:
  0.0 26.1 %copy-start = (bf16[2048,896]{1,0:T(8,128)(2,1)S(1)}, bf16[2048,896]{1,0:T(8,128)(2,1)}, u32[]{:S(2)}) copy-start(bf16[2048,896]{1,0:T(8,128)(2,1)} %param.6) | copy-start | bytes 11010052
  0.0 7.9 %collective-permute-start.1 = (bf16[24,2048]{1,0:T(8,128)(2,1)}, bf16[24,2048]{1,0:T(8,128)(2,1)S(1)}, u32[]{:S(2)}, u32[]{:S(2)}) collective-permute-start(bf16[24,2048]{1,0:T(8,128)(2,1)} %param.4), channel_id=1, source_target_pairs={{0,16},{1,5},{2,18},{3,7},{4,20},{5,1},{6,22},{7,3},{8,24},{9,13},... | collective-permute-start | bytes 294920 | tf_op jit(solution)/shard_map/ppermute | solution.py:95
  3.0 4.8 %collective-permute-start = (bf16[24,2048]{1,0:T(8,128)(2,1)}, bf16[24,2048]{1,0:T(8,128)(2,1)S(1)}, u32[]{:S(2)}, u32[]{:S(2)}) collective-permute-start(bf16[24,2048]{1,0:T(8,128)(2,1)} %param.4), channel_id=1, source_target_pairs={{0,24},{1,7},{2,26},{3,1},{4,28},{5,3},{6,30},{7,5},{8,0},{9,15},{... | collective-permute-start | bytes 294920 | tf_op jit(solution)/shard_map/ppermute | solution.py:95
  4.2 6.0 %collective-permute-start.2 = (bf16[24,2048]{1,0:T(8,128)(2,1)}, bf16[24,2048]{1,0:T(8,128)(2,1)S(1)}, u32[]{:S(2)}, u32[]{:S(2)}) collective-permute-start(bf16[24,2048]{1,0:T(8,128)(2,1)} %param.4), channel_id=1, source_target_pairs={{0,8},{1,3},{2,10},{3,5},{4,12},{5,7},{6,14},{7,1},{8,16},{9,11},{... | collective-permute-start | bytes 294920 | tf_op jit(solution)/shard_map/ppermute | solution.py:95
  10.2 13.3 %collective-permute-start.3 = (bf16[96,2048]{1,0:T(8,128)(2,1)S(1)}, bf16[96,2048]{1,0:T(8,128)(2,1)S(1)}, u32[]{:S(2)}, u32[]{:S(2)}) collective-permute-start(bf16[96,2048]{1,0:T(8,128)(2,1)S(1)} %get-tuple-element.49), channel_id=1, source_target_pairs={{0,6},{1,25},{2,0},{3,27},{4,2},{5,29},{6,4},{7,31},{8,14},{9,1},{... | collective-permute-start | bytes 1179656 | tf_op jit(solution)/shard_map/ppermute | solution.py:96
  11.1 12.5 %collective-permute-start.4 = (bf16[96,2048]{1,0:T(8,128)(2,1)S(1)}, bf16[96,2048]{1,0:T(8,128)(2,1)S(1)}, u32[]{:S(2)}, u32[]{:S(2)}) collective-permute-start(bf16[96,2048]{1,0:T(8,128)(2,1)S(1)} %get-tuple-element.49), channel_id=1, source_target_pairs={{0,4},{1,17},{2,6},{3,19},{4,0},{5,21},{6,2},{7,23},{8,12},{9,25},... | collective-permute-start | bytes 1179656 | tf_op jit(solution)/shard_map/ppermute | solution.py:96
  12.0 12.4 %collective-permute-start.5 = (bf16[96,2048]{1,0:T(8,128)(2,1)S(1)}, bf16[96,2048]{1,0:T(8,128)(2,1)S(1)}, u32[]{:S(2)}, u32[]{:S(2)}) collective-permute-start(bf16[96,2048]{1,0:T(8,128)(2,1)S(1)} %get-tuple-element.49), channel_id=1, source_target_pairs={{0,2},{1,9},{2,4},{3,11},{4,6},{5,13},{6,0},{7,15},{8,10},{9,17},{... | collective-permute-start | bytes 1179656 | tf_op jit(solution)/shard_map/ppermute | solution.py:96
  24.5 1.6 copy-start.3
  26.1 86.3 %collective-permute-start.6 = (bf16[384,2048]{1,0:T(8,128)(2,1)S(1)}, bf16[384,2048]{1,0:T(8,128)(2,1)S(1)}, u32[]{:S(2)}, u32[]{:S(2)}) collective-permute-start(bf16[384,2048]{1,0:T(8,128)(2,1)S(1)} %get-tuple-element.37), channel_id=1, source_target_pairs={{0,1},{1,0},{2,3},{3,2},{4,5},{5,4},{6,7},{7,6},{8,9},{9,8},{10,11... | collective-permute-start | bytes 4718600 | tf_op jit(solution)/shard_map/ppermute | solution.py:97
  113.6 6.5 %copy-start.1 = (bf16[2048,896]{1,0:T(8,128)(2,1)S(1)}, bf16[2048,896]{1,0:T(8,128)(2,1)}, u32[]{:S(2)}) copy-start(bf16[2048,896]{1,0:T(8,128)(2,1)} %param.5) | copy-start | bytes 11010052
  113.7 6.6 %copy-start.4 = (bf16[768,2048]{1,0:T(8,128)(2,1)S(1)}, bf16[768,2048]{1,0:T(8,128)(2,1)}, u32[]{:S(2)}) copy-start(bf16[768,2048]{1,0:T(8,128)(2,1)} %constant_dynamic-update-slice_fusion.11) | copy-start | bytes 9437188
  123.6 29.7 %copy-start.2 = (f32[768,896]{1,0:T(8,128)}, f32[768,896]{1,0:T(8,128)S(1)}, u32[]{:S(2)}) copy-start(f32[768,896]{1,0:T(8,128)S(1)} %fusion.53) | copy-start | bytes 8257540
  123.7 6.9 %collective-permute-start.15 = (f16[48,896]{1,0:T(8,128)(2,1)S(1)}, f16[48,896]{1,0:T(8,128)(2,1)S(1)}, u32[]{:S(2)}, u32[]{:S(2)}) collective-permute-start(f16[48,896]{1,0:T(8,128)(2,1)S(1)} %get-tuple-element.27), channel_id=1, source_target_pairs={{0,32},{32,64},{64,96},{96,128},{128,160},{160,192},{192,224},{224... | collective-permute-start | bytes 258056 | tf_op jit(solution)/shard_map/ppermute | solution.py:57
  124.8 5.9 %collective-permute-start.19 = (f16[48,896]{1,0:T(8,128)(2,1)S(1)}, f16[48,896]{1,0:T(8,128)(2,1)S(1)}, u32[]{:S(2)}, u32[]{:S(2)}) collective-permute-start(f16[48,896]{1,0:T(8,128)(2,1)S(1)} %get-tuple-element.29), channel_id=1, source_target_pairs={{0,224},{32,0},{64,32},{96,64},{128,96},{160,128},{192,160},{224,1... | collective-permute-start | bytes 258056 | tf_op jit(solution)/shard_map/ppermute | solution.py:58
  127.3 6.0 %collective-permute-start.7 = (f16[48,896]{1,0:T(8,128)(2,1)S(1)}, f16[48,896]{1,0:T(8,128)(2,1)S(1)}, u32[]{:S(2)}, u32[]{:S(2)}) collective-permute-start(f16[48,896]{1,0:T(8,128)(2,1)S(1)} %get-tuple-element.17), channel_id=1, source_target_pairs={{0,32},{32,64},{64,96},{96,128},{128,160},{160,192},{192,224},{224... | collective-permute-start | bytes 258056 | tf_op jit(solution)/shard_map/ppermute | solution.py:57
  127.4 6.1 %collective-permute-start.11 = (f16[48,896]{1,0:T(8,128)(2,1)S(1)}, f16[48,896]{1,0:T(8,128)(2,1)S(1)}, u32[]{:S(2)}, u32[]{:S(2)}) collective-permute-start(f16[48,896]{1,0:T(8,128)(2,1)S(1)} %get-tuple-element.19), channel_id=1, source_target_pairs={{0,224},{32,0},{64,32},{96,64},{128,96},{160,128},{192,160},{224,1... | collective-permute-start | bytes 258056 | tf_op jit(solution)/shard_map/ppermute | solution.py:58
  130.8 7.1 %collective-permute-start.20 = (f16[96,896]{1,0:T(8,128)(2,1)S(1)}, f16[96,896]{1,0:T(8,128)(2,1)S(1)}, u32[]{:S(2)}, u32[]{:S(2)}) collective-permute-start(f16[96,896]{1,0:T(8,128)(2,1)S(1)} %pad_maximum_fusion.3), channel_id=1, source_target_pairs={{0,224},{32,0},{64,32},{96,64},{128,96},{160,128},{192,160},{224,1... | collective-permute-start | bytes 516104 | tf_op jit(solution)/shard_map/ppermute | solution.py:67
  133.2 8.4 %collective-permute-start.16 = (f16[96,896]{1,0:T(8,128)(2,1)S(1)}, f16[96,896]{1,0:T(8,128)(2,1)S(1)}, u32[]{:S(2)}, u32[]{:S(2)}) collective-permute-start(f16[96,896]{1,0:T(8,128)(2,1)S(1)} %pad_maximum_fusion.2), channel_id=1, source_target_pairs={{0,32},{32,64},{64,96},{96,128},{128,160},{160,192},{192,224},{224... | collective-permute-start | bytes 516104 | tf_op jit(solution)/shard_map/ppermute | solution.py:66
  133.7 11.3 %collective-permute-start.12 = (f16[96,896]{1,0:T(8,128)(2,1)S(1)}, f16[96,896]{1,0:T(8,128)(2,1)S(1)}, u32[]{:S(2)}, u32[]{:S(2)}) collective-permute-start(f16[96,896]{1,0:T(8,128)(2,1)S(1)} %pad_maximum_fusion.1), channel_id=1, source_target_pairs={{0,224},{32,0},{64,32},{96,64},{128,96},{160,128},{192,160},{224,1... | collective-permute-start | bytes 516104 | tf_op jit(solution)/shard_map/ppermute | solution.py:67
  137.5 7.9 %collective-permute-start.8 = (f16[96,896]{1,0:T(8,128)(2,1)S(1)}, f16[96,896]{1,0:T(8,128)(2,1)S(1)}, u32[]{:S(2)}, u32[]{:S(2)}) collective-permute-start(f16[96,896]{1,0:T(8,128)(2,1)S(1)} %pad_maximum_fusion), channel_id=1, source_target_pairs={{0,32},{32,64},{64,96},{96,128},{128,160},{160,192},{192,224},{224... | collective-permute-start | bytes 516104 | tf_op jit(solution)/shard_map/ppermute | solution.py:66
  141.7 8.2 %collective-permute-start.17 = (f16[96,896]{1,0:T(8,128)(2,1)S(1)}, f16[96,896]{1,0:T(8,128)(2,1)S(1)}, u32[]{:S(2)}, u32[]{:S(2)}) collective-permute-start(f16[96,896]{1,0:T(8,128)(2,1)S(1)} %get-tuple-element.23), channel_id=1, source_target_pairs={{0,32},{32,64},{64,96},{96,128},{128,160},{160,192},{192,224},{224... | collective-permute-start | bytes 516104 | tf_op jit(solution)/shard_map/ppermute | solution.py:66
  141.8 8.1 %collective-permute-start.21 = (f16[96,896]{1,0:T(8,128)(2,1)S(1)}, f16[96,896]{1,0:T(8,128)(2,1)S(1)}, u32[]{:S(2)}, u32[]{:S(2)}) collective-permute-start(f16[96,896]{1,0:T(8,128)(2,1)S(1)} %get-tuple-element.24), channel_id=1, source_target_pairs={{0,224},{32,0},{64,32},{96,64},{128,96},{160,128},{192,160},{224,1... | collective-permute-start | bytes 516104 | tf_op jit(solution)/shard_map/ppermute | solution.py:67
  145.6 7.8 %collective-permute-start.9 = (f16[96,896]{1,0:T(8,128)(2,1)S(1)}, f16[96,896]{1,0:T(8,128)(2,1)S(1)}, u32[]{:S(2)}, u32[]{:S(2)}) collective-permute-start(f16[96,896]{1,0:T(8,128)(2,1)S(1)} %get-tuple-element.13), channel_id=1, source_target_pairs={{0,32},{32,64},{64,96},{96,128},{128,160},{160,192},{192,224},{224... | collective-permute-start | bytes 516104 | tf_op jit(solution)/shard_map/ppermute | solution.py:66
  145.6 7.7 %collective-permute-start.13 = (f16[96,896]{1,0:T(8,128)(2,1)S(1)}, f16[96,896]{1,0:T(8,128)(2,1)S(1)}, u32[]{:S(2)}, u32[]{:S(2)}) collective-permute-start(f16[96,896]{1,0:T(8,128)(2,1)S(1)} %get-tuple-element.14), channel_id=1, source_target_pairs={{0,224},{32,0},{64,32},{96,64},{128,96},{160,128},{192,160},{224,1... | collective-permute-start | bytes 516104 | tf_op jit(solution)/shard_map/ppermute | solution.py:67
  150.0 7.4 %collective-permute-start.18 = (f16[96,896]{1,0:T(8,128)(2,1)S(1)}, f16[96,896]{1,0:T(8,128)(2,1)S(1)}, u32[]{:S(2)}, u32[]{:S(2)}) collective-permute-start(f16[96,896]{1,0:T(8,128)(2,1)S(1)} %get-tuple-element.21), channel_id=1, source_target_pairs={{0,32},{32,64},{64,96},{96,128},{128,160},{160,192},{192,224},{224... | collective-permute-start | bytes 516104 | tf_op jit(solution)/shard_map/ppermute | solution.py:66
  150.1 7.3 %collective-permute-start.22 = (f16[96,896]{1,0:T(8,128)(2,1)S(1)}, f16[96,896]{1,0:T(8,128)(2,1)S(1)}, u32[]{:S(2)}, u32[]{:S(2)}) collective-permute-start(f16[96,896]{1,0:T(8,128)(2,1)S(1)} %get-tuple-element.22), channel_id=1, source_target_pairs={{0,224},{32,0},{64,32},{96,64},{128,96},{160,128},{192,160},{224,1... | collective-permute-start | bytes 516104 | tf_op jit(solution)/shard_map/ppermute | solution.py:67
  154.2 6.9 %collective-permute-start.10 = (f16[96,896]{1,0:T(8,128)(2,1)}, f16[96,896]{1,0:T(8,128)(2,1)}, u32[]{:S(2)}, u32[]{:S(2)}) collective-permute-start(f16[96,896]{1,0:T(8,128)(2,1)} %get-tuple-element.11), channel_id=1, source_target_pairs={{0,32},{32,64},{64,96},{96,128},{128,160},{160,192},{192,224},{224... | collective-permute-start | bytes 516104 | tf_op jit(solution)/shard_map/ppermute | solution.py:66
  154.2 6.9 %collective-permute-start.14 = (f16[96,896]{1,0:T(8,128)(2,1)}, f16[96,896]{1,0:T(8,128)(2,1)}, u32[]{:S(2)}, u32[]{:S(2)}) collective-permute-start(f16[96,896]{1,0:T(8,128)(2,1)} %get-tuple-element.12), channel_id=1, source_target_pairs={{0,224},{32,0},{64,32},{96,64},{128,96},{160,128},{192,160},{224,1... | collective-permute-start | bytes 516104 | tf_op jit(solution)/shard_map/ppermute | solution.py:67
  161.1 38.9 %copy-start.5 = (bf16[896,2048]{1,0:T(8,128)(2,1)S(1)}, bf16[896,2048]{1,0:T(8,128)(2,1)}, u32[]{:S(2)}) copy-start(bf16[896,2048]{1,0:T(8,128)(2,1)} %param.7) | copy-start | bytes 11010052
  162.7 17.7 %collective-permute-start.23 = (bf16[96,896]{1,0:T(8,128)(2,1)S(1)}, bf16[96,896]{1,0:T(8,128)(2,1)S(1)}, u32[]{:S(2)}, u32[]{:S(2)}) collective-permute-start(bf16[96,896]{1,0:T(8,128)(2,1)S(1)} %get-tuple-element.10), channel_id=1, source_target_pairs={{0,32},{32,64},{64,96},{96,128},{128,160},{160,192},{192,224},{224... | collective-permute-start | bytes 516104 | tf_op jit(solution)/shard_map/ppermute | solution.py:81
  173.0 7.5 %collective-permute-start.24 = (bf16[96,896]{1,0:T(8,128)(2,1)S(1)}, bf16[96,896]{1,0:T(8,128)(2,1)S(1)}, u32[]{:S(2)}, u32[]{:S(2)}) collective-permute-start(bf16[96,896]{1,0:T(8,128)(2,1)S(1)} %get-tuple-element.10), channel_id=1, source_target_pairs={{0,224},{32,0},{64,32},{96,64},{128,96},{160,128},{192,160},{224,1... | collective-permute-start | bytes 516104 | tf_op jit(solution)/shard_map/ppermute | solution.py:82
  180.5 7.1 %collective-permute-start.25 = (bf16[96,896]{1,0:T(8,128)(2,1)S(1)}, bf16[96,896]{1,0:T(8,128)(2,1)S(1)}, u32[]{:S(2)}, u32[]{:S(2)}) collective-permute-start(bf16[96,896]{1,0:T(8,128)(2,1)S(1)} %collective-permute-done.23), channel_id=1, source_target_pairs={{0,32},{32,64},{64,96},{96,128},{128,160},{160,192},{192,224},{224... | collective-permute-start | bytes 516104 | tf_op jit(solution)/shard_map/ppermute | solution.py:81
  180.5 7.1 %collective-permute-start.26 = (bf16[96,896]{1,0:T(8,128)(2,1)S(1)}, bf16[96,896]{1,0:T(8,128)(2,1)S(1)}, u32[]{:S(2)}, u32[]{:S(2)}) collective-permute-start(bf16[96,896]{1,0:T(8,128)(2,1)S(1)} %collective-permute-done.24), channel_id=1, source_target_pairs={{0,224},{32,0},{64,32},{96,64},{128,96},{160,128},{192,160},{224,1... | collective-permute-start | bytes 516104 | tf_op jit(solution)/shard_map/ppermute | solution.py:82
  187.6 6.6 %collective-permute-start.27 = (bf16[96,896]{1,0:T(8,128)(2,1)S(1)}, bf16[96,896]{1,0:T(8,128)(2,1)S(1)}, u32[]{:S(2)}, u32[]{:S(2)}) collective-permute-start(bf16[96,896]{1,0:T(8,128)(2,1)S(1)} %collective-permute-done.25), channel_id=1, source_target_pairs={{0,32},{32,64},{64,96},{96,128},{128,160},{160,192},{192,224},{224... | collective-permute-start | bytes 516104 | tf_op jit(solution)/shard_map/ppermute | solution.py:81
  187.6 6.7 %collective-permute-start.28 = (bf16[96,896]{1,0:T(8,128)(2,1)S(1)}, bf16[96,896]{1,0:T(8,128)(2,1)S(1)}, u32[]{:S(2)}, u32[]{:S(2)}) collective-permute-start(bf16[96,896]{1,0:T(8,128)(2,1)S(1)} %collective-permute-done.26), channel_id=1, source_target_pairs={{0,224},{32,0},{64,32},{96,64},{128,96},{160,128},{192,160},{224,1... | collective-permute-start | bytes 516104 | tf_op jit(solution)/shard_map/ppermute | solution.py:82
  194.2 5.8 %collective-permute-start.29 = (bf16[48,896]{1,0:T(8,128)(2,1)S(1)}, bf16[48,896]{1,0:T(8,128)(2,1)S(1)}, u32[]{:S(2)}, u32[]{:S(2)}) collective-permute-start(bf16[48,896]{1,0:T(8,128)(2,1)S(1)} %slice.123), channel_id=1, source_target_pairs={{0,32},{32,64},{64,96},{96,128},{128,160},{160,192},{192,224},{224... | collective-permute-start | bytes 258056 | tf_op jit(solution)/shard_map/ppermute | solution.py:85
  194.3 5.7 %collective-permute-start.30 = (bf16[48,896]{1,0:T(8,128)(2,1)S(1)}, bf16[48,896]{1,0:T(8,128)(2,1)S(1)}, u32[]{:S(2)}, u32[]{:S(2)}) collective-permute-start(bf16[48,896]{1,0:T(8,128)(2,1)S(1)} %slice.124), channel_id=1, source_target_pairs={{0,224},{32,0},{64,32},{96,64},{128,96},{160,128},{192,160},{224,1... | collective-permute-start | bytes 258056 | tf_op jit(solution)/shard_map/ppermute | solution.py:85
  203.7 3.5 %collective-permute-start.31 = (bf16[384,2048]{1,0:T(8,128)(2,1)S(1)}, bf16[384,2048]{1,0:T(8,128)(2,1)S(1)}, u32[]{:S(2)}, u32[]{:S(2)}) collective-permute-start(bf16[384,2048]{1,0:T(8,128)(2,1)S(1)} %slice.149), channel_id=1, source_target_pairs={{0,1},{1,0},{2,3},{3,2},{4,5},{5,4},{6,7},{7,6},{8,9},{9,8},{10,11... | collective-permute-start | bytes 4718600 | tf_op jit(solution)/shard_map/ppermute | solution.py:108
  208.0 11.5 %collective-permute-start.32 = (bf16[96,2048]{1,0:T(8,128)(2,1)S(1)}, bf16[96,2048]{1,0:T(8,128)(2,1)S(1)}, u32[]{:S(2)}, u32[]{:S(2)}) collective-permute-start(bf16[96,2048]{1,0:T(8,128)(2,1)S(1)} %get-tuple-element.31), channel_id=1, source_target_pairs={{0,2},{1,9},{2,4},{3,11},{4,6},{5,13},{6,0},{7,15},{8,10},{9,17},{... | collective-permute-start | bytes 1179656 | tf_op jit(solution)/shard_map/ppermute | solution.py:111
  210.0 13.2 %collective-permute-start.34 = (bf16[96,2048]{1,0:T(8,128)(2,1)S(1)}, bf16[96,2048]{1,0:T(8,128)(2,1)S(1)}, u32[]{:S(2)}, u32[]{:S(2)}) collective-permute-start(bf16[96,2048]{1,0:T(8,128)(2,1)S(1)} %get-tuple-element.32), channel_id=1, source_target_pairs={{0,6},{1,25},{2,0},{3,27},{4,2},{5,29},{6,4},{7,31},{8,14},{9,1},{... | collective-permute-start | bytes 1179656 | tf_op jit(solution)/shard_map/ppermute | solution.py:111
  210.1 13.0 %collective-permute-start.33 = (bf16[96,2048]{1,0:T(8,128)(2,1)S(1)}, bf16[96,2048]{1,0:T(8,128)(2,1)S(1)}, u32[]{:S(2)}, u32[]{:S(2)}) collective-permute-start(bf16[96,2048]{1,0:T(8,128)(2,1)S(1)} %get-tuple-element.33), channel_id=1, source_target_pairs={{0,4},{1,17},{2,6},{3,19},{4,0},{5,21},{6,2},{7,23},{8,12},{9,25},... | collective-permute-start | bytes 1179656 | tf_op jit(solution)/shard_map/ppermute | solution.py:111
  223.4 5.9 %collective-permute-start.35 = (bf16[24,2048]{1,0:T(8,128)(2,1)S(1)}, bf16[24,2048]{1,0:T(8,128)(2,1)S(1)}, u32[]{:S(2)}, u32[]{:S(2)}) collective-permute-start(bf16[24,2048]{1,0:T(8,128)(2,1)S(1)} %get-tuple-element.34), channel_id=1, source_target_pairs={{0,8},{1,3},{2,10},{3,5},{4,12},{5,7},{6,14},{7,1},{8,16},{9,11},{... | collective-permute-start | bytes 294920 | tf_op jit(solution)/shard_map/ppermute | solution.py:111
  223.6 6.3 %collective-permute-start.37 = (bf16[24,2048]{1,0:T(8,128)(2,1)S(1)}, bf16[24,2048]{1,0:T(8,128)(2,1)S(1)}, u32[]{:S(2)}, u32[]{:S(2)}) collective-permute-start(bf16[24,2048]{1,0:T(8,128)(2,1)S(1)} %get-tuple-element.35), channel_id=1, source_target_pairs={{0,24},{1,7},{2,26},{3,1},{4,28},{5,3},{6,30},{7,5},{8,0},{9,15},{... | collective-permute-start | bytes 294920 | tf_op jit(solution)/shard_map/ppermute | solution.py:111
  226.7 6.1 %collective-permute-start.36 = (bf16[24,2048]{1,0:T(8,128)(2,1)S(1)}, bf16[24,2048]{1,0:T(8,128)(2,1)S(1)}, u32[]{:S(2)}, u32[]{:S(2)}) collective-permute-start(bf16[24,2048]{1,0:T(8,128)(2,1)S(1)} %get-tuple-element.36), channel_id=1, source_target_pairs={{0,16},{1,5},{2,18},{3,7},{4,20},{5,1},{6,22},{7,3},{8,24},{9,13},... | collective-permute-start | bytes 294920 | tf_op jit(solution)/shard_map/ppermute | solution.py:111
